TPU v7x, 32 devices: a whole 2x2x4 slice. The times are simulated.
32 devices in a mesh: dp: 4 (over x, core), seq: 8 (over z, y).
Axes of the slice: x: 2, y: 2, z: 4, core: 2. Of those that a mesh axis runs over, the one named last changes fastest.
Arguments:
- encoded: bfloat16 [4, 1024, 2048], P('dp', 'seq'), may hold values from -6 to 6
- cotangents: bfloat16 [2, 4, 1024, 2, 2048], P(None, 'dp', 'seq'), may hold values from -6 to 6
- weights: bfloat16 [2, 2, 2048, 2048], P(None, None, None, 'dp'), may hold values from -0.125 to 0.125
Outputs:
- input_grad: bfloat16 [4, 1024, 2048], P('dp', 'seq')
- weight_grad: float32 [2048, 2, 2, 2048], P('seq', None, None, 'dp')
All inputs are finite; a program needn't handle non-finite values.
Results may differ from a plain program's by a relative error of at most 0.001.
Values may be sent and summed in bfloat16 or wider, within the bound.
A program may use at most 128 MiB of HBM per device.

v0:
```python
import jax
import jax.numpy as jnp
from jax import lax
from jax.sharding import PartitionSpec as P


def local(encoded, cotangents, weights):
    gathered = lax.all_gather(encoded, "dp", axis=0, tiled=True)
    spread = lax.all_to_all(cotangents, "dp", split_axis=4, concat_axis=1, tiled=True)
    layer_total = spread.shape[0]
    feat_width = gathered.shape[2]
    flat_rows = gathered.reshape(-1, feat_width)
    grad_rows = spread.reshape(layer_total, flat_rows.shape[0], 2, spread.shape[4])
    token_total = flat_rows.shape[0] * lax.axis_size("seq")
    norm_factor = 1.0 / jnp.sqrt(jnp.float32(token_total))
    local_rows = feat_width // lax.axis_size("seq")
    input_sum = jnp.zeros(encoded.shape, jnp.float32)
    pieces = []
    for layer_idx in range(layer_total):
        layer_grad = grad_rows[layer_idx]
        layer_weight = weights[layer_idx]
        partial_input = jnp.einsum(
            "tce,cde->td", layer_grad, layer_weight, preferred_element_type=jnp.float32
        )
        input_sum = input_sum + lax.psum_scatter(
            partial_input.reshape(gathered.shape), "dp", scatter_dimension=0, tiled=True
        )

        def layer_term(first_row, row_count, layer_grad=layer_grad):
            return (
                jnp.einsum("td,tce->dce", flat_rows, layer_grad, preferred_element_type=jnp.float32)
                * norm_factor
            )

        pieces.append(
            lax.psum_scatter(
                layer_term(jnp.int32(0), lax.axis_size("seq") * local_rows),
                "seq",
                scatter_dimension=0,
                tiled=True,
            )
        )
    weight_grad = jnp.stack(pieces, axis=1)
    return (input_sum.astype(jnp.bfloat16), weight_grad)


def solution(mesh):
    return jax.shard_map(
        local,
        mesh=mesh,
        in_specs=(
            P("dp", "seq", None),
            P(None, "dp", "seq", None, None),
            P(None, None, None, "dp"),
        ),
        out_specs=(P("dp", "seq", None), P("seq", None, None, "dp")),
        check_vma=False,
    )
```

profile of v0, /device:TPU:0, one launch (start us, length us, event | category | flops | bytes accessed | tf_op | source)
XLA Modules:
  0.0 434.6 jit_solution(2029279036402782658)
XLA Ops:
  7.2 8.5 %copy.13 = bf16[2,1,128,2,2048]{2,3,0,1,4:T(2,128)(2,1)} copy(bf16[2,1,128,2,2048]{4,3,2,1,0:T(2,128)(2,1)} %param.4) | data formatting | bytes 4194304 | tf_op args[1]
  15.7 4.2 all-to-all-start
  19.9 0.0 all-gather.2.cloned.1.call-start
  19.9 0.7 all-gather.2.cloned.1.call-update
  20.6 0.0 reduce-scatter.8.cloned.1.call-start
  20.7 36.2 %all-to-all-done = bf16[2,1,128,2,2048]{2,3,0,1,4:T(2,128)(2,1)S(1)} async-done(((bf16[2,1,128,2,2048]{2,3,0,1,4:T(2,128)(2,1)}), bf16[2,1,128,2,2048]{2,3,0,1,4:T(2,128)(2,1)S(1)}, u32[]{:S(2)}, u32[]{:S(2)}) %all-to-all-start) | async-done | bytes 2097184 | tf_op jit(solution)/shard_map/all_to_all | solution.py:9
  56.8 4.6 %copy.15 = bf16[2,1,128,2,4,512]{5,2,3,4,1,0:T(8,128)(2,1)} copy(bf16[2,1,128,2,4,512]{2,3,0,5,4,1:T(2,128)(2,1)S(1)} %bitcast.37) | data formatting | bytes 4194304 | tf_op jit(solution)/shard_map/all_to_all | solution.py:9
  61.4 0.0 copy-start
  61.4 5.0 %fusion = f32[4,128,2048,1]{2,1,3,0:T(8,128)S(1)} fusion(bf16[2,2,2048,512]{3,2,1,0:T(8,128)(2,1)} %param.5, bf16[2,4,1,128,2,512]{5,3,4,1,2,0:T(8,128)(2,1)} %bitcast.38), kind=kOutput, calls=%fused_computation.3 | convolution fusion | flops 2147483648 | bytes 9437184 | tf_op jit(solution)/shard_map/tce,cde->td/dot_general | solution.py:22
  66.4 0.0 copy-done
  66.4 6.5 %bitcast_add_fusion = f32[4,128,2048]{2,1,0:T(8,128)} fusion(f32[4,128,2048,1]{2,1,3,0:T(8,128)S(1)} %fusion, bf16[2,2,2048,512]{3,2,1,0:T(8,128)(2,1)} %param.5, bf16[2,4,1,128,2,512]{5,3,4,1,2,0:T(8,128)(2,1)S(1)} %bitcast.39), kind=kOutput, calls=%fused_computation.2 | convolution fusion | flops 2148532224 | bytes 13631488 | tf_op jit(solution)/shard_map/tce,cde->td/dot_general | solution.py:22
  72.9 0.0 reduce-scatter.8.cloned.1.call-update
  73.0 0.0 reduce-scatter.6.cloned.1.call-start
  73.0 0.2 fusion.12
  73.2 0.1 copy.18
  73.3 0.0 all-gather.2.cloned.1.call-done
  73.3 7.5 %convolution_multiply_fusion = f32[2048,2,512]{2,0,1:T(8,128)} fusion(bf16[512,2048,1]{1,0,2:T(8,128)(2,1)} %bitcast.45, bf16[512,2,512]{2,0,1:T(8,128)(2,1)S(1)} %bitcast.41), kind=kOutput, calls=%fused_computation | convolution fusion | flops 2149580800 | bytes 11534336 | tf_op jit(solution)/shard_map/td,tce->dce/dot_general | solution.py:31
  80.8 0.0 copy-start.1
  80.8 0.0 reduce-scatter.6.cloned.1.call-update
  80.8 0.0 reduce-scatter.4.cloned.1.call-start
  80.9 0.1 copy.17
  81.0 1.7 copy-done.1
  82.7 5.6 %convolution_multiply_fusion.1 = f32[2048,2,512]{2,0,1:T(8,128)} fusion(bf16[512,2048,1]{1,0,2:T(8,128)(2,1)S(1)} %bitcast.46, bf16[512,2,512]{2,0,1:T(8,128)(2,1)S(1)} %bitcast.42), kind=kOutput, calls=%fused_computation.1 | convolution fusion | flops 2149580800 | bytes 11534336 | tf_op jit(solution)/shard_map/td,tce->dce/dot_general | solution.py:31
  88.3 0.0 reduce-scatter.4.cloned.1.call-update
  88.4 30.4 %reduce-scatter.8.cloned.1.call-done = f32[1,128,2048]{2,1,0:T(8,128)} async-done(((f32[4,128,2048]{2,1,0:T(8,128)}), f32[1,128,2048]{2,1,0:T(8,128)}) %reduce-scatter.8.cloned.1.call-update) | async-done | bytes 1048592 | tf_op jit(solution)/shard_map/reduce_scatter | solution.py:25
  118.7 2.1 convert_element_type.3
  120.8 151.0 %reduce-scatter.6.cloned.1.call-done = f32[256,2,512]{2,0,1:T(8,128)} async-done(((f32[2048,2,512]{2,0,1:T(8,128)}), f32[256,2,512]{2,0,1:T(8,128)}) %reduce-scatter.6.cloned.1.call-update) | async-done | bytes 1048592 | tf_op jit(solution)/shard_map/reduce_scatter | solution.py:36
  271.8 151.5 %reduce-scatter.4.cloned.1.call-done = f32[256,2,512]{2,0,1:T(8,128)} async-done(((f32[2048,2,512]{2,0,1:T(8,128)}), f32[256,2,512]{2,0,1:T(8,128)}) %reduce-scatter.4.cloned.1.call-update) | async-done | bytes 1048592 | tf_op jit(solution)/shard_map/reduce_scatter | solution.py:36
  423.4 1.7 pad_maximum_fusion
  425.1 2.9 copy.19
Async XLA Ops:
  15.7 41.1 %all-to-all-start = ((bf16[2,1,128,2,2048]{2,3,0,1,4:T(2,128)(2,1)}), bf16[2,1,128,2,2048]{2,3,0,1,4:T(2,128)(2,1)S(1)}, u32[]{:S(2)}, u32[]{:S(2)}) async-start(bf16[2,1,128,2,2048]{2,3,0,1,4:T(2,128)(2,1)} %copy.13), calls=%async_computation | async-start | bytes 4194304 | tf_op jit(solution)/shard_map/all_to_all | solution.py:9
  19.9 53.4 %all-gather.2.cloned.1.call-start = ((), (), s32[]{:S(2)}) async-start(), calls=%async_computation.4 | async-start | bytes 2621440 | tf_op jit(solution)/shard_map/all_gather | solution.py:8
  20.6 98.1 %reduce-scatter.8.cloned.1.call-start = ((), (), s32[]{:S(2)}) async-start(), calls=%async_computation.7 | async-start | bytes 5242880 | tf_op jit(solution)/shard_map/reduce_scatter | solution.py:25
  61.4 5.0 %copy-start = (bf16[2,1,128,2,4,512]{5,2,3,4,1,0:T(8,128)(2,1)S(1)}, bf16[2,1,128,2,4,512]{5,2,3,4,1,0:T(8,128)(2,1)}, u32[]{:S(2)}) copy-start(bf16[2,1,128,2,4,512]{5,2,3,4,1,0:T(8,128)(2,1)} %copy.15) | copy-start | bytes 6291460
  73.0 198.9 %reduce-scatter.6.cloned.1.call-start = ((), (), s32[]{:S(2)}) async-start(), calls=%async_computation.6 | async-start | bytes 9437184 | tf_op jit(solution)/shard_map/reduce_scatter | solution.py:36
  80.8 1.9 copy-start.1
  80.8 342.6 %reduce-scatter.4.cloned.1.call-start = ((), (), s32[]{:S(2)}) async-start(), calls=%async_computation.5 | async-start | bytes 9437184 | tf_op jit(solution)/shard_map/reduce_scatter | solution.py:36
Sparse Core Ops, SparseCore 0:
  22.3 35.8 all-gather.1
  73.1 45.6 reduce-scatter.7
  122.8 148.9 reduce-scatter.5
  275.3 148.0 reduce-scatter.3
where the time goes:
time: 435 us
  waiting for transfers between devices  370 us (85%)
  matrix products  24.6 us (6%)
  local copies, waits for them, and re-layouts  18.2 us (4%)
  between operations  13.8 us (3%)
    reduce_scatter x2, waiting for transfers between devices, local(): lax.psum_scatter(layer_term(jnp.int32(0), lax.axis_size('seq') * local_ro...  303 us
    all_to_all x1, waiting for transfers between devices, local(): lax.all_to_all(cotangents, 'dp', split_axis=4, concat_axis=1, tiled=True)  36.2 us
    reduce_scatter x1, waiting for transfers between devices, local(): lax.psum_scatter(partial_input.reshape(gathered.shape), 'dp', scatter_dim...  30.4 us
    unnamed x6, local copies, waits for them, and re-layouts  13.2 us
    dot_general x2, matrix products, layer_term(): jnp.einsum('td,tce->dce', flat_rows, layer_grad, preferred_element_type=j...  13.1 us
    dot_general x2, matrix products, local(): jnp.einsum('tce,cde->td', layer_grad, layer_weight, preferred_element_typ...  11.5 us
  transfers between devices with their start and end apart: 5, of which 4 were waited for; matrix products, arithmetic and copies ran while one was open for 7% of the time, Pallas kernels for 0%

commit v1 on v0

v1 whole, which is shorter than its diff:
```python
import jax
import jax.numpy as jnp
from jax import lax
from jax.sharding import PartitionSpec as P

F32 = jnp.float32
BF16 = jnp.bfloat16
TOP = 2.0**30


def encode(x):
    square = x * x
    return (square * x * jnp.abs(x)).astype(BF16)


def decode(y):
    y = y.astype(F32)
    root = jnp.sqrt(jnp.sqrt(jnp.abs(y)))
    return jnp.where(y < 0, -root, root)


def local(encoded, cotangents, weights):
    ndp, nseq = lax.axis_size("dp"), lax.axis_size("seq")
    nz = nseq // 2
    me, seq = lax.axis_index("dp"), lax.axis_index("seq")
    y, z = seq % 2, seq // 2
    layers, _, rows, parts, units = cotangents.shape
    feats = encoded.shape[2]
    dl = feats // nseq
    el = units // ndp
    lc = layers * parts
    tokens = rows * nseq * ndp

    def swap_dp(a, k):
        return lax.ppermute(a, "dp", [(i, i ^ k) for i in range(ndp)])

    def swap_y(a):
        return lax.ppermute(a, "seq", [(i, i ^ 1) for i in range(nseq)])

    peak = lax.pmax(
        jnp.stack([jnp.max(jnp.abs(encoded)), jnp.max(jnp.abs(cotangents))]).astype(F32),
        ("dp", "seq"),
    )
    peak = jnp.maximum(peak, 1e-30)
    inv = 1.0 / peak
    down = (peak[0] * peak[1]) * (tokens / TOP) * (1.0 / jnp.sqrt(F32(tokens)))

    blocks = cotangents[:, 0].reshape(layers, rows, parts, ndp, el)
    blocks = blocks.transpose(3, 0, 2, 1, 4).reshape(ndp, lc, rows, el)

    enc = encoded[0].reshape(rows, nz, 2, dl).transpose(2, 1, 0, 3)
    enc_own = lax.dynamic_index_in_dim(enc, y, 0, keepdims=False)
    enc_far = swap_y(lax.dynamic_index_in_dim(enc, 1 - y, 0, keepdims=False))
    enc0 = jnp.stack([enc_own, enc_far])
    enc_src = [enc0, swap_dp(enc0, 1), swap_dp(enc0, 2)]
    enc_src.append(swap_dp(enc_src[1], 2))
    enc_all = jnp.concatenate(enc_src, 0).transpose(1, 0, 2, 3).reshape(nz, 2 * ndp * rows, dl)

    near = []
    for k in range(ndp):
        b = lax.dynamic_index_in_dim(blocks, me ^ k, 0, keepdims=False)
        near.append(b if k == 0 else swap_dp(b, k))
    far = [swap_y(b) for b in near]
    cot_all = jnp.stack([jnp.stack([n, f]) for n, f in zip(near, far)])
    cot_all = cot_all.transpose(2, 0, 1, 3, 4).reshape(lc, 2 * ndp * rows, el)

    factor = inv[0] * (TOP / tokens)

    def term(b):
        e = lax.dynamic_index_in_dim(enc_all, jnp.clip(b, 0, nz - 1), 0, keepdims=False)
        t = jnp.einsum("td,cte->dce", e, cot_all, preferred_element_type=F32)
        return t * factor * inv[1]

    right = left = None
    for s in range(nz - 1):
        r = term(z + (nz - 1 - s))
        l = term(z - (nz - 1 - s))
        if s:
            r = r + decode(right)
            l = l + decode(left)
        rp, lp = [], []
        for q in range(min(s + 1, nz - 1)):
            for yy in range(2):
                rp.append((q * 2 + yy, (q + 1) * 2 + yy))
                lp.append(((nz - 1 - q) * 2 + yy, (nz - 2 - q) * 2 + yy))
        right = lax.ppermute(encode(r), "seq", rp)
        left = lax.ppermute(encode(l), "seq", lp)
    wg = term(z)
    if nz > 1:
        wg = wg + decode(right) + decode(left)
    weight_grad = (wg * down).reshape(dl, layers, parts, el)

    def part(k):
        w = weights.reshape(lc, feats, el)
        return jnp.einsum("cte,cde->td", near[k], w, preferred_element_type=F32)

    held = [part(k) for k in range(ndp)]
    bit = 1
    while bit < ndp:
        held = [
            a + b
            for a, b in zip(
                [held[k] for k in range(len(held)) if not (k & 1)],
                [swap_dp(held[k], bit) for k in range(len(held)) if k & 1],
            )
        ]
        bit *= 2
    input_grad = held[0].astype(BF16)[None]
    return (input_grad, weight_grad)


def solution(mesh):
    return jax.shard_map(
        local,
        mesh=mesh,
        in_specs=(
            P("dp", "seq", None),
            P(None, "dp", "seq", None, None),
            P(None, None, None, "dp"),
        ),
        out_specs=(P("dp", "seq", None), P("seq", None, None, "dp")),
        check_vma=False,
    )
```

time: 435 us -> 226 us (0.52)
  waiting for transfers between devices: 370 us -> 72.1 us
  blocking collectives: 0 us -> 45.6 us
  starting transfers between devices: 4.33 us -> 27.5 us
  matrix products: 24.6 us -> 41.3 us
  between operations: 13.8 us -> 2.86 us
  other arithmetic: 3.79 us -> 14 us
    reduce_scatter x3 -> x0, waiting for transfers between devices: 333 us -> none  [the longest x2 303 us: local(): lax.psum_scatter(layer_term(jnp.int32(0), lax.axis_size('seq') * local_ro...]
    ppermute x0 -> x20, waiting for transfers between devices: none -> 72.1 us  [the longest x3 31.3 us: local(): right = lax.ppermute(encode(r), 'seq', rp)]
    pmax x0 -> x1, blocking collectives: none -> 45.6 us  [local(): lax.pmax(jnp.stack([jnp.max(jnp.abs(encoded)), jnp.max(jnp.abs(cotangents...]
    all_to_all x1 -> x0, waiting for transfers between devices: 36.2 us -> none  [local(): lax.all_to_all(cotangents, 'dp', split_axis=4, concat_axis=1, tiled=True)]
    ppermute x0 -> x20, starting transfers between devices: none -> 27.5 us  [the longest x3 11.5 us: local(): right = lax.ppermute(encode(r), 'seq', rp)]
    dot_general x4 -> x11, matrix products: 24.6 us -> 41.3 us  [the longest x7 24.4 us: term(): t = jnp.einsum('td,cte->dce', e, cot_all, preferred_element_type=F32)]
    unnamed x6 -> x18, local copies, waits for them, and re-layouts: 13.2 us -> 6.2 us
    reduce_max x0 -> x2, other arithmetic: none -> 5.72 us  [the longest x1 4.98 us: local(): jnp.max(jnp.abs(cotangents))]
  transfers between devices with their start and end apart: 5 -> 20, of which waited for: 4 -> 8; matrix products, arithmetic and copies ran while one was open for 7% -> 24% of each run, Pallas kernels for 0% -> 0%
where the time goes in v1:
time: 226 us; the launch traced here: 225 us
  waiting for transfers between devices  72.1 us (32%)
  blocking collectives  45.6 us (20%)
  matrix products  41.3 us (18%)
  starting transfers between devices  27.5 us (12%)
  local copies, waits for them, and re-layouts  21.5 us (10%)
  other arithmetic  14 us (6%)
  between operations  2.86 us (1%)
    pmax x1, blocking collectives, local(): lax.pmax(jnp.stack([jnp.max(jnp.abs(encoded)), jnp.max(jnp.abs(cotangents...  45.6 us
    ppermute x3, waiting for transfers between devices, local(): right = lax.ppermute(encode(r), 'seq', rp)  31.3 us
    dot_general x7, matrix products, term(): t = jnp.einsum('td,cte->dce', e, cot_all, preferred_element_type=F32)  24.4 us
    ppermute x5, waiting for transfers between devices, swap_y(): return lax.ppermute(a, 'seq', [(i, i ^ 1) for i in range(nseq)])  22.7 us
    dot_general x4, matrix products, part(): return jnp.einsum('cte,cde->td', near[k], w, preferred_element_type=F32)  16.9 us
    ppermute x3, waiting for transfers between devices, local(): left = lax.ppermute(encode(l), 'seq', lp)  13 us
    ppermute x3, starting transfers between devices, local(): right = lax.ppermute(encode(r), 'seq', rp)  11.5 us
    ppermute x9, starting transfers between devices, swap_dp(): return lax.ppermute(a, 'dp', [(i, i ^ k) for i in range(ndp)])  8.14 us
  transfers between devices with their start and end apart: 20, of which 8 were waited for; matrix products, arithmetic and copies ran while one was open for 24% of the time, Pallas kernels for 0%

profile of v1, /device:TPU:0, one launch (start us, length us, event | category | flops | bytes accessed | tf_op | source)
XLA Modules:
  0.0 224.9 jit_solution(10661408982189503567)
XLA Ops:
  0.6 3.2 %reshape_squeeze.6 = bf16[2,128,2,4,512]{4,3,2,1,0:T(4,128)(2,1)S(1)} reshape(bf16[2,1,128,2,2048]{4,3,2,1,0:T(2,128)(2,1)} %param.4) | data formatting | bytes 4194304 | tf_op jit(solution)/shard_map/reshape;squeeze | solution.py:48
  3.8 2.0 copy.12
  5.8 2.8 %dynamic-slice_bitcast_fusion.2 = (bf16[4,128,512]{2,1,0:T(8,128)(2,1)}, bf16[4,128,512]{2,1,0:T(8,128)(2,1)}, bf16[4,128,512]{2,1,0:T(8,128)(2,1)}, bf16[1,4,128,512]{3,2,1,0:T(8,128)(2,1)S(1)}) fusion(bf16[4,4,128,512]{3,2,1,0:T(8,128)(2,1)} %bitcast.122, s32[]{:T(128)S(6)} %select_n.59, s32[]{:T(128)S(6)} %select_n.61, s32[]{:T(128)S(6)} %select_n.60, ...), kind=kLoop, calls=%fused_computation.89 | loop fusion | bytes 4194320 | tf_op jit(solution)/shard_map/jit(dynamic_index_in_dim)/squeeze | solution.py:61
  8.7 2.4 %collective-permute-start.3 = (bf16[4,128,512]{2,1,0:T(8,128)(2,1)}, bf16[4,128,512]{2,1,0:T(8,128)(2,1)}, u32[]{:S(2)}, u32[]{:S(2)}) collective-permute-start(bf16[4,128,512]{2,1,0:T(8,128)(2,1)} %get-tuple-element.11), channel_id=1, source_target_pairs={{0,24},{8,16},{16,8},{24,0},{1,25},{9,17},{17,9},{25,1},{2,26},{10... | collective-permute-start | bytes 1572872 | tf_op jit(solution)/shard_map/ppermute | solution.py:35
  16.4 5.0 %abs_reduce_fusion = bf16[]{:T(256)} fusion(bf16[2,1,128,2,2048]{4,3,2,1,0:T(2,128)(2,1)S(1)} %copy-done), kind=kLoop, calls=%fused_computation.61 | loop fusion | flops 2097151 | bytes 2097154 | tf_op jit(solution)/shard_map/reduce_max | solution.py:41
  24.5 45.6 %pmax.7 = f32[2]{0:T(128)S(1)} all-reduce(f32[2]{0:T(128)S(1)} %maximum_convert_fusion), channel_id=1, replica_groups=mesh['dp'=4,'seq'=8] {'dp','seq'}, use_global_device_ids=true, to_apply=%region_2.3 | all-reduce | flops 2 | bytes 16 | tf_op jit(solution)/shard_map/pmax | solution.py:40
  71.0 2.3 %collective-permute-start.8 = (bf16[2,4,128,256]{2,3,0,1:T(8,128)(2,1)}, bf16[2,4,128,256]{2,3,0,1:T(8,128)(2,1)}, u32[]{:S(2)}, u32[]{:S(2)}) collective-permute-start(bf16[2,4,128,256]{2,3,0,1:T(8,128)(2,1)} %pad_maximum_fusion), channel_id=1, source_target_pairs={{0,16},{8,24},{16,0},{24,8},{1,17},{9,25},{17,1},{25,9},{2,18},{10... | collective-permute-start | bytes 1572872 | tf_op jit(solution)/shard_map/ppermute | solution.py:35
  81.3 5.1 %collective-permute-done.8 = bf16[2,4,128,256]{2,3,0,1:T(8,128)(2,1)} collective-permute-done((bf16[2,4,128,256]{2,3,0,1:T(8,128)(2,1)}, bf16[2,4,128,256]{2,3,0,1:T(8,128)(2,1)}, u32[]{:S(2)}, u32[]{:S(2)}) %collective-permute-start.8) | collective-permute-done | bytes 524320 | tf_op jit(solution)/shard_map/ppermute | solution.py:35
  87.5 3.3 %collective-permute-done.13 = bf16[4,128,512]{2,1,0:T(8,128)(2,1)S(1)} collective-permute-done((bf16[4,128,512]{2,1,0:T(8,128)(2,1)}, bf16[4,128,512]{2,1,0:T(8,128)(2,1)S(1)}, u32[]{:S(2)}, u32[]{:S(2)}) %collective-permute-start.13) | collective-permute-done | bytes 524320 | tf_op jit(solution)/shard_map/ppermute | solution.py:38
  92.0 10.1 %collective-permute-done.12 = bf16[4,128,512]{2,1,0:T(8,128)(2,1)S(1)} collective-permute-done((bf16[4,128,512]{2,1,0:T(8,128)(2,1)}, bf16[4,128,512]{2,1,0:T(8,128)(2,1)S(1)}, u32[]{:S(2)}, u32[]{:S(2)}) %collective-permute-start.12) | collective-permute-done | bytes 524320 | tf_op jit(solution)/shard_map/ppermute | solution.py:38
  103.2 9.3 %collective-permute-done.11 = bf16[4,128,512]{2,1,0:T(8,128)(2,1)S(1)} collective-permute-done((bf16[4,128,512]{2,1,0:T(8,128)(2,1)}, bf16[4,128,512]{2,1,0:T(8,128)(2,1)S(1)}, u32[]{:S(2)}, u32[]{:S(2)}) %collective-permute-start.11) | collective-permute-done | bytes 524320 | tf_op jit(solution)/shard_map/ppermute | solution.py:38
  114.3 2.4 %copy.18 = bf16[4,4,2,128,512]{4,3,2,1,0:T(8,128)(2,1)} copy(bf16[4,4,2,128,512]{4,3,0,2,1:T(8,128)(2,1)S(1)} %maximum_bitcast_fusion) | data formatting | bytes 8388608 | tf_op jit(solution)/shard_map/transpose | solution.py:65
  116.8 2.6 %copy.16 = bf16[4,8,128,256]{3,2,1,0:T(8,128)(2,1)} copy(bf16[4,8,128,256]{2,3,1,0:T(8,128)(2,1)S(1)} %bitcast.131) | data formatting | bytes 4194304 | tf_op jit(solution)/shard_map/transpose | solution.py:57
  119.4 4.5 %fusion.14 = bf16[256,4,512]{2,0,1:T(8,128)(2,1)S(1)} fusion(bf16[4,1024,512]{2,1,0:T(8,128)(2,1)} %bitcast.124, f32[]{:T(128)} %bitcast.38, f32[]{:T(128)} %bitcast.37, bf16[4,1024,256]{2,1,0:T(8,128)(2,1)} %bitcast.132, s32[]{:T(128)S(6)} %min.25), kind=kOutput, calls=%fused_computation.43 | convolution fusion | flops 1077411840 | bytes 5768196 | tf_op jit(solution)/shard_map/td,cte->dce/dot_general | solution.py:71
  123.9 2.6 %collective-permute-start.14 = (bf16[256,4,512]{2,0,1:T(8,128)(2,1)S(1)}, bf16[256,4,512]{2,0,1:T(8,128)(2,1)S(1)}, u32[]{:S(2)}, u32[]{:S(2)}) collective-permute-start(bf16[256,4,512]{2,0,1:T(8,128)(2,1)S(1)} %fusion.14), channel_id=1, source_target_pairs={{0,2},{1,3},{8,10},{9,11},{16,18},{17,19},{24,26},{25,27}} | collective-permute-start | bytes 3145736 | tf_op jit(solution)/shard_map/ppermute | solution.py:86
  126.5 6.5 %convolution_bitcast_fusion = f32[128,2048]{1,0:T(8,128)S(1)} fusion(bf16[4,128,512]{2,1,0:T(8,128)(2,1)} %collective-permute-done.3, bf16[4,2048,512]{2,1,0:T(8,128)(2,1)} %bitcast.116), kind=kOutput, calls=%fused_computation.25 | convolution fusion | flops 1073741824 | bytes 9961472 | tf_op jit(solution)/shard_map/cte,cde->td/dot_general | solution.py:95
  133.1 2.2 fusion.25
  136.0 3.8 %convolution_bitcast_fusion.2 = f32[128,2048]{1,0:T(8,128)S(1)} fusion(bf16[4,128,512]{2,1,0:T(8,128)(2,1)} %collective-permute-done, bf16[4,2048,512]{2,1,0:T(8,128)(2,1)S(1)} %bitcast.119), kind=kOutput, calls=%fused_computation.27 | convolution fusion | flops 1073741824 | bytes 9961472 | tf_op jit(solution)/shard_map/cte,cde->td/dot_general | solution.py:95
  140.2 7.9 %collective-permute-done.14 = bf16[256,4,512]{2,0,1:T(8,128)(2,1)S(1)} collective-permute-done((bf16[256,4,512]{2,0,1:T(8,128)(2,1)S(1)}, bf16[256,4,512]{2,0,1:T(8,128)(2,1)S(1)}, u32[]{:S(2)}, u32[]{:S(2)}) %collective-permute-start.14) | collective-permute-done | bytes 1048608 | tf_op jit(solution)/shard_map/ppermute | solution.py:86
  148.1 3.3 %fusion.17 = bf16[256,4,512]{2,0,1:T(8,128)(2,1)S(1)} fusion(bf16[256,4,512]{2,0,1:T(8,128)(2,1)S(1)} %collective-permute-done.14, bf16[4,1024,512]{2,1,0:T(8,128)(2,1)S(1)} %bitcast.126, f32[]{:T(128)} %bitcast.38, f32[]{:T(128)} %bitcast.37, bf16[4,1024,256]{2,1,0:T(8,128)(2,1)S(1)} %bitcast.134, s32[]{:T(128)S(6)} %min.24), kind=kOutput, calls=%fused_computation.46 | convolution fusion | flops 1080557568 | bytes 6815756 | tf_op jit(solution)/shard_map/td,cte->dce/dot_general | solution.py:71
  151.4 4.5 %collective-permute-start.15 = (bf16[256,4,512]{2,0,1:T(8,128)(2,1)S(1)}, bf16[256,4,512]{2,0,1:T(8,128)(2,1)S(1)}, u32[]{:S(2)}, u32[]{:S(2)}) collective-permute-start(bf16[256,4,512]{2,0,1:T(8,128)(2,1)S(1)} %fusion.17), channel_id=1, source_target_pairs={{0,2},{1,3},{2,4},{3,5},{8,10},{9,11},{10,12},{11,13},{16,18},{17,... | collective-permute-start | bytes 3145736 | tf_op jit(solution)/shard_map/ppermute | solution.py:86
  155.9 3.3 %fusion.28 = bf16[256,4,512]{2,0,1:T(8,128)(2,1)S(1)} fusion(bf16[256,4,512]{2,0,1:T(8,128)(2,1)S(1)} %collective-permute-done.17, bf16[4,1024,512]{2,1,0:T(8,128)(2,1)S(1)} %bitcast.127, f32[]{:T(128)} %bitcast.38, f32[]{:T(128)} %bitcast.37, bf16[4,1024,256]{2,1,0:T(8,128)(2,1)S(1)} %bitcast.135, s32[]{:T(128)S(6)} %min.27), kind=kOutput, calls=%fused_computation.57 | convolution fusion | flops 1080557568 | bytes 6815756 | tf_op jit(solution)/shard_map/td,cte->dce/dot_general | solution.py:71
  160.2 3.8 %fusion = f32[128,2048]{1,0:T(8,128)S(1)} fusion(f32[128,2048]{1,0:T(8,128)S(1)} %collective-permute-done.4, bf16[4,128,512]{2,1,0:T(8,128)(2,1)} %collective-permute-done.2, bf16[4,2048,512]{2,1,0:T(8,128)(2,1)S(1)} %bitcast.120), kind=kOutput, calls=%fused_computation.29 | convolution fusion | flops 1074003968 | bytes 11010048 | tf_op jit(solution)/shard_map/cte,cde->td/dot_general | solution.py:95
  164.7 12.1 %collective-permute-done.15 = bf16[256,4,512]{2,0,1:T(8,128)(2,1)S(1)} collective-permute-done((bf16[256,4,512]{2,0,1:T(8,128)(2,1)S(1)}, bf16[256,4,512]{2,0,1:T(8,128)(2,1)S(1)}, u32[]{:S(2)}, u32[]{:S(2)}) %collective-permute-start.15) | collective-permute-done | bytes 1048608 | tf_op jit(solution)/shard_map/ppermute | solution.py:86
  176.8 3.3 %fusion.20 = bf16[256,4,512]{2,0,1:T(8,128)(2,1)S(1)} fusion(bf16[256,4,512]{2,0,1:T(8,128)(2,1)S(1)} %collective-permute-done.15, f32[]{:T(128)} %bitcast.38, f32[]{:T(128)} %bitcast.37, bf16[4,1024,512]{2,1,0:T(8,128)(2,1)S(1)} %bitcast.128, bf16[4,1024,256]{2,1,0:T(8,128)(2,1)S(1)} %bitcast.136, s32[]{:T(128)S(6)} %min.23), kind=kOutput, calls=%fused_computation.49 | convolution fusion | flops 1080557568 | bytes 6815756 | tf_op jit(solution)/shard_map/td,cte->dce/dot_general | solution.py:71
  180.1 4.5 %collective-permute-start.16 = (bf16[256,4,512]{2,0,1:T(8,128)(2,1)S(1)}, bf16[256,4,512]{2,0,1:T(8,128)(2,1)S(1)}, u32[]{:S(2)}, u32[]{:S(2)}) collective-permute-start(bf16[256,4,512]{2,0,1:T(8,128)(2,1)S(1)} %fusion.20), channel_id=1, source_target_pairs={{0,2},{1,3},{2,4},{3,5},{4,6},{5,7},{8,10},{9,11},{10,12},{11,13},... | collective-permute-start | bytes 3145736 | tf_op jit(solution)/shard_map/ppermute | solution.py:86
  184.6 3.3 %fusion.31 = bf16[256,4,512]{2,0,1:T(8,128)(2,1)S(1)} fusion(bf16[256,4,512]{2,0,1:T(8,128)(2,1)S(1)} %collective-permute-done.18, f32[]{:T(128)} %bitcast.38, f32[]{:T(128)} %bitcast.37, bf16[4,1024,512]{2,1,0:T(8,128)(2,1)S(1)} %bitcast.129, bf16[4,1024,256]{2,1,0:T(8,128)(2,1)S(1)} %bitcast.137, s32[]{:T(128)S(6)} %min.26), kind=kOutput, calls=%fused_computation.60 | convolution fusion | flops 1080557568 | bytes 6815756 | tf_op jit(solution)/shard_map/td,cte->dce/dot_general | solution.py:71
  189.5 2.8 %convolution_bitcast_fusion.3 = f32[128,2048]{1,0:T(8,128)S(1)} fusion(bf16[4,2048,512]{2,1,0:T(8,128)(2,1)S(1)} %bitcast.121, bf16[1,4,128,512]{3,2,1,0:T(8,128)(2,1)S(1)} %get-tuple-element.13), kind=kOutput, calls=%fused_computation.28 | convolution fusion | flops 1073741824 | bytes 9961472 | tf_op jit(solution)/shard_map/cte,cde->td/dot_general | solution.py:95
  193.3 11.3 %collective-permute-done.16 = bf16[256,4,512]{2,0,1:T(8,128)(2,1)S(1)} collective-permute-done((bf16[256,4,512]{2,0,1:T(8,128)(2,1)S(1)}, bf16[256,4,512]{2,0,1:T(8,128)(2,1)S(1)}, u32[]{:S(2)}, u32[]{:S(2)}) %collective-permute-start.16) | collective-permute-done | bytes 1048608 | tf_op jit(solution)/shard_map/ppermute | solution.py:86
  204.6 13.0 %collective-permute-done.19 = bf16[256,4,512]{2,0,1:T(8,128)(2,1)S(1)} collective-permute-done((bf16[256,4,512]{2,0,1:T(8,128)(2,1)S(1)}, bf16[256,4,512]{2,0,1:T(8,128)(2,1)S(1)}, u32[]{:S(2)}, u32[]{:S(2)}) %collective-permute-start.19) | collective-permute-done | bytes 1048608 | tf_op jit(solution)/shard_map/ppermute | solution.py:87
  217.5 4.5 %fusion.23 = f32[256,4,512]{2,0,1:T(8,128)S(1)} fusion(bf16[256,4,512]{2,0,1:T(8,128)(2,1)S(1)} %collective-permute-done.16, bf16[256,4,512]{2,0,1:T(8,128)(2,1)S(1)} %collective-permute-done.19, f32[]{:T(128)} %bitcast.51, f32[]{:T(128)} %bitcast.38, f32[]{:T(128)} %bitcast.37, bf16[4,1024,512]{2,1,0:T(8,128)(2,1)S(1)} %bitcast.130, ...), kind=kOutput, calls=%fused_computation.52 | convolution fusion | flops 1081606144 | bytes 8912912 | tf_op jit(solution)/shard_map/td,cte->dce/dot_general | solution.py:71
  222.0 2.9 %copy.25 = f32[256,2,2,512]{3,2,1,0:T(2,128)} copy(f32[256,2,2,512]{3,0,2,1:T(8,128)S(1)} %bitcast.139) | data formatting | bytes 4194304
  (58 shorter events, 26.0 us)
Async XLA Ops:
  5.8 7.7 %copy-start.3 = (bf16[1,128,2048]{2,1,0:T(8,128)(2,1)S(1)}, bf16[1,128,2048]{2,1,0:T(8,128)(2,1)}, u32[]{:S(2)}) copy-start(bf16[1,128,2048]{2,1,0:T(8,128)(2,1)} %param.3) | copy-start | bytes 1572868
  5.8 10.6 %copy-start = (bf16[2,1,128,2,2048]{4,3,2,1,0:T(2,128)(2,1)S(1)}, bf16[2,1,128,2,2048]{4,3,2,1,0:T(2,128)(2,1)}, u32[]{:S(2)}) copy-start(bf16[2,1,128,2,2048]{4,3,2,1,0:T(2,128)(2,1)} %param.4) | copy-start | bytes 6291460
  8.7 62.3 %collective-permute-start.3 = (bf16[4,128,512]{2,1,0:T(8,128)(2,1)}, bf16[4,128,512]{2,1,0:T(8,128)(2,1)}, u32[]{:S(2)}, u32[]{:S(2)}) collective-permute-start(bf16[4,128,512]{2,1,0:T(8,128)(2,1)} %get-tuple-element.11), channel_id=1, source_target_pairs={{0,24},{8,16},{16,8},{24,0},{1,25},{9,17},{17,9},{25,1},{2,26},{10... | collective-permute-start | bytes 1572872 | tf_op jit(solution)/shard_map/ppermute | solution.py:35
  11.0 64.8 %collective-permute-start.2 = (bf16[4,128,512]{2,1,0:T(8,128)(2,1)}, bf16[4,128,512]{2,1,0:T(8,128)(2,1)}, u32[]{:S(2)}, u32[]{:S(2)}) collective-permute-start(bf16[4,128,512]{2,1,0:T(8,128)(2,1)} %get-tuple-element.12), channel_id=1, source_target_pairs={{0,16},{8,24},{16,0},{24,8},{1,17},{9,25},{17,1},{25,9},{2,18},{10... | collective-permute-start | bytes 1572872 | tf_op jit(solution)/shard_map/ppermute | solution.py:35
  11.6 64.8 %collective-permute-start = (bf16[4,128,512]{2,1,0:T(8,128)(2,1)}, bf16[4,128,512]{2,1,0:T(8,128)(2,1)}, u32[]{:S(2)}, u32[]{:S(2)}) collective-permute-start(bf16[4,128,512]{2,1,0:T(8,128)(2,1)} %get-tuple-element.10), channel_id=1, source_target_pairs={{0,8},{8,0},{16,24},{24,16},{1,9},{9,1},{17,25},{25,17},{2,10},{10... | collective-permute-start | bytes 1572872 | tf_op jit(solution)/shard_map/ppermute | solution.py:35
  11.7 66.3 %collective-permute-start.10 = (bf16[4,128,512]{2,1,0:T(8,128)(2,1)S(1)}, bf16[4,128,512]{2,1,0:T(8,128)(2,1)}, u32[]{:S(2)}, u32[]{:S(2)}) collective-permute-start(bf16[4,128,512]{2,1,0:T(8,128)(2,1)S(1)} %bitcast.123), channel_id=1, source_target_pairs={{0,1},{1,0},{2,3},{3,2},{4,5},{5,4},{6,7},{7,6},{8,9},{9,8},{10,11... | collective-permute-start | bytes 1572872 | tf_op jit(solution)/shard_map/ppermute | solution.py:38
  16.2 54.0 %collective-permute-start.6 = (bf16[4,128,256]{1,2,0:T(8,128)(2,1)}, bf16[4,128,256]{1,2,0:T(8,128)(2,1)S(1)}, u32[]{:S(2)}, u32[]{:S(2)}) collective-permute-start(bf16[4,128,256]{1,2,0:T(8,128)(2,1)} %dynamic-slice_bitcast_fusion.3), channel_id=1, source_target_pairs={{0,1},{1,0},{2,3},{3,2},{4,5},{5,4},{6,7},{7,6},{8,9},{9,8},{10,11... | collective-permute-start | bytes 786440 | tf_op jit(solution)/shard_map/ppermute | solution.py:38
  71.0 8.7 %collective-permute-start.7 = (bf16[2,4,128,256]{2,3,0,1:T(8,128)(2,1)}, bf16[2,4,128,256]{2,3,0,1:T(8,128)(2,1)S(1)}, u32[]{:S(2)}, u32[]{:S(2)}) collective-permute-start(bf16[2,4,128,256]{2,3,0,1:T(8,128)(2,1)} %pad_maximum_fusion), channel_id=1, source_target_pairs={{0,8},{8,0},{16,24},{24,16},{1,9},{9,1},{17,25},{25,17},{2,10},{10... | collective-permute-start | bytes 1572872 | tf_op jit(solution)/shard_map/ppermute | solution.py:35
  71.0 15.4 %collective-permute-start.8 = (bf16[2,4,128,256]{2,3,0,1:T(8,128)(2,1)}, bf16[2,4,128,256]{2,3,0,1:T(8,128)(2,1)}, u32[]{:S(2)}, u32[]{:S(2)}) collective-permute-start(bf16[2,4,128,256]{2,3,0,1:T(8,128)(2,1)} %pad_maximum_fusion), channel_id=1, source_target_pairs={{0,16},{8,24},{16,0},{24,8},{1,17},{9,25},{17,1},{25,9},{2,18},{10... | collective-permute-start | bytes 1572872 | tf_op jit(solution)/shard_map/ppermute | solution.py:35
  75.8 15.0 %collective-permute-start.13 = (bf16[4,128,512]{2,1,0:T(8,128)(2,1)}, bf16[4,128,512]{2,1,0:T(8,128)(2,1)S(1)}, u32[]{:S(2)}, u32[]{:S(2)}) collective-permute-start(bf16[4,128,512]{2,1,0:T(8,128)(2,1)} %collective-permute-done.3), channel_id=1, source_target_pairs={{0,1},{1,0},{2,3},{3,2},{4,5},{5,4},{6,7},{7,6},{8,9},{9,8},{10,11... | collective-permute-start | bytes 1572872 | tf_op jit(solution)/shard_map/ppermute | solution.py:38
  76.4 25.7 %collective-permute-start.12 = (bf16[4,128,512]{2,1,0:T(8,128)(2,1)}, bf16[4,128,512]{2,1,0:T(8,128)(2,1)S(1)}, u32[]{:S(2)}, u32[]{:S(2)}) collective-permute-start(bf16[4,128,512]{2,1,0:T(8,128)(2,1)} %collective-permute-done.2), channel_id=1, source_target_pairs={{0,1},{1,0},{2,3},{3,2},{4,5},{5,4},{6,7},{7,6},{8,9},{9,8},{10,11... | collective-permute-start | bytes 1572872 | tf_op jit(solution)/shard_map/ppermute | solution.py:38
  78.0 34.5 %collective-permute-start.11 = (bf16[4,128,512]{2,1,0:T(8,128)(2,1)}, bf16[4,128,512]{2,1,0:T(8,128)(2,1)S(1)}, u32[]{:S(2)}, u32[]{:S(2)}) collective-permute-start(bf16[4,128,512]{2,1,0:T(8,128)(2,1)} %collective-permute-done), channel_id=1, source_target_pairs={{0,1},{1,0},{2,3},{3,2},{4,5},{5,4},{6,7},{7,6},{8,9},{9,8},{10,11... | collective-permute-start | bytes 1572872 | tf_op jit(solution)/shard_map/ppermute | solution.py:38
  79.7 37.0 %collective-permute-start.9 = (bf16[2,4,128,256]{2,3,0,1:T(8,128)(2,1)S(1)}, bf16[2,4,128,256]{2,3,0,1:T(8,128)(2,1)S(1)}, u32[]{:S(2)}, u32[]{:S(2)}) collective-permute-start(bf16[2,4,128,256]{2,3,0,1:T(8,128)(2,1)S(1)} %collective-permute-done.7), channel_id=1, source_target_pairs={{0,16},{8,24},{16,0},{24,8},{1,17},{9,25},{17,1},{25,9},{2,18},{10... | collective-permute-start | bytes 1572872 | tf_op jit(solution)/shard_map/ppermute | solution.py:35
  119.4 13.7 %copy-start.2 = (bf16[4,8,128,256]{3,2,1,0:T(8,128)(2,1)S(1)}, bf16[4,8,128,256]{3,2,1,0:T(8,128)(2,1)}, u32[]{:S(2)}) copy-start(bf16[4,8,128,256]{3,2,1,0:T(8,128)(2,1)} %copy.16) | copy-start | bytes 6291460
  123.9 24.2 %collective-permute-start.14 = (bf16[256,4,512]{2,0,1:T(8,128)(2,1)S(1)}, bf16[256,4,512]{2,0,1:T(8,128)(2,1)S(1)}, u32[]{:S(2)}, u32[]{:S(2)}) collective-permute-start(bf16[256,4,512]{2,0,1:T(8,128)(2,1)S(1)} %fusion.14), channel_id=1, source_target_pairs={{0,2},{1,3},{8,10},{9,11},{16,18},{17,19},{24,26},{25,27}} | collective-permute-start | bytes 3145736 | tf_op jit(solution)/shard_map/ppermute | solution.py:86
  126.5 6.6 %copy-start.1 = (bf16[4,4,2,128,512]{4,3,2,1,0:T(8,128)(2,1)S(1)}, bf16[4,4,2,128,512]{4,3,2,1,0:T(8,128)(2,1)}, u32[]{:S(2)}) copy-start(bf16[4,4,2,128,512]{4,3,2,1,0:T(8,128)(2,1)} %copy.18) | copy-start | bytes 12582916
  126.5 9.5 %slice-start = ((s8[8388608]{0:T(1024)(128)(4,1)}), s8[4194304]{0:T(1024)(128)(4,1)S(1)}, s32[]{:S(2)}) async-start(s8[8388608]{0:T(1024)(128)(4,1)} %bitcast.117), calls=%async_computation | async-start | bytes 8388608
  133.0 3.0 %slice-start.1 = ((s8[8388608]{0:T(1024)(128)(4,1)}), s8[4194304]{0:T(1024)(128)(4,1)S(1)}, s32[]{:S(2)}) async-start(s8[8388608]{0:T(1024)(128)(4,1)} %bitcast.117), calls=%async_computation.1 | async-start | bytes 8388608
  133.0 27.2 %collective-permute-start.4 = (f32[128,2048]{1,0:T(8,128)S(1)}, f32[128,2048]{1,0:T(8,128)S(1)}, u32[]{:S(2)}, u32[]{:S(2)}) collective-permute-start(f32[128,2048]{1,0:T(8,128)S(1)} %convolution_bitcast_fusion), channel_id=1, source_target_pairs={{0,8},{8,0},{16,24},{24,16},{1,9},{9,1},{17,25},{25,17},{2,10},{10... | collective-permute-start | bytes 3145736 | tf_op jit(solution)/shard_map/ppermute | solution.py:35
  135.2 20.7 %collective-permute-start.17 = (bf16[256,4,512]{2,0,1:T(8,128)(2,1)S(1)}, bf16[256,4,512]{2,0,1:T(8,128)(2,1)S(1)}, u32[]{:S(2)}, u32[]{:S(2)}) collective-permute-start(bf16[256,4,512]{2,0,1:T(8,128)(2,1)S(1)} %fusion.25), channel_id=1, source_target_pairs={{6,4},{7,5},{14,12},{15,13},{22,20},{23,21},{30,28},{31,29}} | collective-permute-start | bytes 3145736 | tf_op jit(solution)/shard_map/ppermute | solution.py:87
  139.8 52.4 %collective-permute-start.1 = (f32[128,2048]{1,0:T(8,128)S(1)}, f32[128,2048]{1,0:T(8,128)S(1)}, u32[]{:S(2)}, u32[]{:S(2)}) collective-permute-start(f32[128,2048]{1,0:T(8,128)S(1)} %convolution_bitcast_fusion.2), channel_id=1, source_target_pairs={{0,8},{8,0},{16,24},{24,16},{1,9},{9,1},{17,25},{25,17},{2,10},{10... | collective-permute-start | bytes 3145736 | tf_op jit(solution)/shard_map/ppermute | solution.py:35
  151.4 25.4 %collective-permute-start.15 = (bf16[256,4,512]{2,0,1:T(8,128)(2,1)S(1)}, bf16[256,4,512]{2,0,1:T(8,128)(2,1)S(1)}, u32[]{:S(2)}, u32[]{:S(2)}) collective-permute-start(bf16[256,4,512]{2,0,1:T(8,128)(2,1)S(1)} %fusion.17), channel_id=1, source_target_pairs={{0,2},{1,3},{2,4},{3,5},{8,10},{9,11},{10,12},{11,13},{16,18},{17,... | collective-permute-start | bytes 3145736 | tf_op jit(solution)/shard_map/ppermute | solution.py:86
  159.2 25.4 %collective-permute-start.18 = (bf16[256,4,512]{2,0,1:T(8,128)(2,1)S(1)}, bf16[256,4,512]{2,0,1:T(8,128)(2,1)S(1)}, u32[]{:S(2)}, u32[]{:S(2)}) collective-permute-start(bf16[256,4,512]{2,0,1:T(8,128)(2,1)S(1)} %fusion.28), channel_id=1, source_target_pairs={{6,4},{7,5},{4,2},{5,3},{14,12},{15,13},{12,10},{13,11},{22,20},{2... | collective-permute-start | bytes 3145736 | tf_op jit(solution)/shard_map/ppermute | solution.py:87
  164.0 28.3 %collective-permute-start.5 = (f32[128,2048]{1,0:T(8,128)S(1)}, f32[128,2048]{1,0:T(8,128)S(1)}, u32[]{:S(2)}, u32[]{:S(2)}) collective-permute-start(f32[128,2048]{1,0:T(8,128)S(1)} %fusion), channel_id=1, source_target_pairs={{0,16},{8,24},{16,0},{24,8},{1,17},{9,25},{17,1},{25,9},{2,18},{10... | collective-permute-start | bytes 3145736 | tf_op jit(solution)/shard_map/ppermute | solution.py:35
  180.1 24.5 %collective-permute-start.16 = (bf16[256,4,512]{2,0,1:T(8,128)(2,1)S(1)}, bf16[256,4,512]{2,0,1:T(8,128)(2,1)S(1)}, u32[]{:S(2)}, u32[]{:S(2)}) collective-permute-start(bf16[256,4,512]{2,0,1:T(8,128)(2,1)S(1)} %fusion.20), channel_id=1, source_target_pairs={{0,2},{1,3},{2,4},{3,5},{4,6},{5,7},{8,10},{9,11},{10,12},{11,13},... | collective-permute-start | bytes 3145736 | tf_op jit(solution)/shard_map/ppermute | solution.py:86
  187.9 29.6 %collective-permute-start.19 = (bf16[256,4,512]{2,0,1:T(8,128)(2,1)S(1)}, bf16[256,4,512]{2,0,1:T(8,128)(2,1)S(1)}, u32[]{:S(2)}, u32[]{:S(2)}) collective-permute-start(bf16[256,4,512]{2,0,1:T(8,128)(2,1)S(1)} %fusion.31), channel_id=1, source_target_pairs={{6,4},{7,5},{4,2},{5,3},{2,0},{3,1},{14,12},{15,13},{12,10},{13,11... | collective-permute-start | bytes 3145736 | tf_op jit(solution)/shard_map/ppermute | solution.py:87

commit v2 on v0

v2 whole, which is shorter than its diff:
```python
import jax
import jax.numpy as jnp
from jax import lax
from jax.experimental import pallas as pl
from jax.experimental.pallas import tpu as pltpu
from jax.sharding import PartitionSpec as P

F32 = jnp.float32
BF16 = jnp.bfloat16
TOP = 2.0**30
MESH = pl.DeviceIdType.MESH


def encode(x):
    square = x * x
    return (square * x * jnp.abs(x)).astype(BF16)


def decode(y):
    y = y.astype(F32)
    root = jnp.sqrt(jnp.sqrt(jnp.abs(y)))
    return jnp.where(y < 0, -root, root)


def kernel(ndp, nseq, cot, enc, w, ig, wg, near, far, encs, recv, send, wv, igs, igr, xs, xr, pks, pkr, pkz,
           wsem, ss_cot, rs_cot, ss_enc, rs_enc, ss_z, rs_z, ss_ig, rs_ig, ss_pk, rs_pk, ss_pz, rs_pz):
    nz = nseq // 2
    _, lc, rows, el = cot.shape
    dl = enc.shape[2]
    feats = w.shape[1]
    tokens = rows * nseq * ndp
    me, seq = lax.axis_index("dp"), lax.axis_index("seq")
    y, z = seq % 2, seq // 2
    pair = me + 1 - 2 * (me % 2)
    across = me + 2 - 4 * (me // 2)
    dps = (me, pair, across, 3 - me)
    ypeer = z * 2 + 1 - y

    def dp_dev(k):
        return (dps[k], seq)

    y_dev = (me, ypeer)

    def z_dev(zz):
        return (me, zz * 2 + y)

    def rcopy(src, dst, s, r, dev):
        return pltpu.make_async_remote_copy(
            src_ref=src, dst_ref=dst, send_sem=s, recv_sem=r, device_id=dev, device_id_type=MESH
        )

    barrier = pltpu.get_barrier_semaphore()
    for k in (1, 2, 3):
        pl.semaphore_signal(barrier, inc=1, device_id=dp_dev(k), device_id_type=MESH)
    pl.semaphore_signal(barrier, inc=1, device_id=y_dev, device_id_type=MESH)

    @pl.loop(1, nz)
    def _(d):
        pl.semaphore_signal(barrier, inc=1, device_id=z_dev((z + d) % nz), device_id_type=MESH)

    pl.semaphore_wait(barrier, 4 + nz - 1)

    wcopy = pltpu.make_async_copy(w, wv, wsem)

    def enc_copy(slot, src, dev):
        return rcopy(src, encs.at[slot], ss_enc.at[slot], rs_enc.at[slot], dev)

    e_y = enc_copy(1, enc.at[1 - y], y_dev)
    e_own2 = enc_copy(4, enc.at[y], dp_dev(2))
    e_own1 = enc_copy(2, enc.at[y], dp_dev(1))
    e_far2 = enc_copy(5, encs.at[1], dp_dev(2))
    e_far1 = enc_copy(3, encs.at[1], dp_dev(1))
    e_on1 = enc_copy(6, encs.at[4], dp_dev(1))
    e_on1f = enc_copy(7, encs.at[5], dp_dev(1))

    def near_ref(c, k):
        return cot.at[me, c] if k == 0 else near.at[c, k - 1]

    def dp_copy(c, k):
        return rcopy(cot.at[dps[k], c], near.at[c, k - 1], ss_cot.at[c, k], rs_cot.at[c, k], dp_dev(k))

    def y_copy(c, k):
        return rcopy(near_ref(c, k), far.at[c, k], ss_cot.at[c, 4 + k], rs_cot.at[c, 4 + k], y_dev)

    e_y.start()
    e_own2.start()
    y_copy(0, 0).start()
    dp_copy(0, 1).start()
    dp_copy(0, 2).start()
    dp_copy(0, 3).start()
    e_own1.start()
    wcopy.start()
    for c in range(1, lc):
        for k in (1, 2, 3):
            dp_copy(c, k).start()

    def cot_peak(i, m):
        return jnp.maximum(m, jnp.max(jnp.abs(cot[i // lc, i % lc].astype(F32)), axis=0, keepdims=True))

    def enc_peak(i, m):
        return jnp.maximum(m, jnp.max(jnp.abs(enc[i // nz, i % nz].astype(F32)), axis=0, keepdims=True))

    mc = jnp.max(lax.fori_loop(0, ndp * lc, cot_peak, jnp.zeros((1, el), F32)), axis=1, keepdims=True)
    me_ = jnp.max(lax.fori_loop(0, 2 * nz, enc_peak, jnp.zeros((1, rows), F32)), axis=1, keepdims=True)
    upper = lax.broadcasted_iota(jnp.int32, (8, 128), 0) < 4
    tile = jnp.where(upper, jnp.broadcast_to(me_, (8, 128)), jnp.broadcast_to(mc, (8, 128)))

    def pk_copy(i, dev):
        return rcopy(pks.at[i], pkr.at[i], ss_pk.at[i], rs_pk.at[i], dev)

    def pk_stage(i):
        pk_copy(i, None if i < 0 else (dp_dev(1), dp_dev(2), y_dev)[i]).wait_recv()
        pks[i + 1] = jnp.maximum(pks[i], pkr[i])

    pks[0] = tile
    pk_copy(0, dp_dev(1)).start()

    dp_copy(0, 1).wait_recv()
    y_copy(0, 1).start()
    pk_stage(0)
    pk_copy(1, dp_dev(2)).start()
    e_y.wait_recv()
    e_far2.start()
    e_far1.start()
    e_own2.wait_recv()
    e_on1.start()
    for k in (2, 3):
        dp_copy(0, k).wait_recv()
        y_copy(0, k).start()
    pk_stage(1)
    pk_copy(2, y_dev).start()

    def forward(c):
        for k in range(4):
            if k:
                dp_copy(c, k).wait_recv()
            y_copy(c, k).start()

    def pz_copy(d):
        return rcopy(pks.at[3], pkz.at[d], ss_pz.at[d], rs_pz.at[d], z_dev((z + d) % nz))

    e_far2.wait_recv()
    e_on1f.start()
    forward(1)
    pk_stage(2)
    pkz[0] = pks[3]

    @pl.loop(1, nz)
    def _(d):
        pz_copy(d).start()

    e_own1.wait_recv()
    e_far1.wait_recv()
    e_on1.wait_recv()
    e_on1f.wait_recv()

    @pl.loop(1, nz)
    def _(d):
        pz_copy(d).wait_recv()

    def pz_max(d, m):
        return jnp.maximum(m, pkz[d])

    peak = jnp.maximum(lax.fori_loop(1, nz, pz_max, pkz[0]), 1e-30)
    peak_e, peak_c = peak[0:1, 0:1], peak[4:5, 0:1]
    up_e = (TOP / tokens) / peak_e
    up_c = 1.0 / peak_c
    norm = 1.0 / jnp.sqrt(jnp.full((1, 1), tokens, F32))
    down = peak_e * peak_c * (tokens / TOP) * norm

    def term(b, c):
        lhs = jnp.concatenate([enc[y, b]] + [encs[s, b] for s in range(1, 2 * ndp)], axis=1)
        pieces = []
        for k in range(ndp):
            pieces += [cot[me, c] if k == 0 else near[c, k - 1], far[c, k]]
        rhs = jnp.concatenate(pieces, axis=0)
        t = jnp.dot(lhs, rhs, preferred_element_type=F32)
        return t * up_e * up_c

    lower = z < nz // 2
    way = jnp.where(lower, 0, 1)
    m = jnp.where(lower, z, nz - 1 - z)

    def z_copy(c, d, j, slot):
        return rcopy(send.at[c, slot], recv.at[c, d, j], ss_z.at[c, slot], rs_z.at[c, d, j], z_dev(z + 1 - 2 * d))

    def move(c, d, j, slot, has_prev):
        block = jnp.where(d == 0, nz - 1 - j, j)

        @pl.when(has_prev)
        def _():
            z_copy(c, d, j, slot).wait_recv()
            send[c, slot] = encode(term(block, c) + decode(recv[c, d, j]))

        @pl.when(jnp.logical_not(has_prev))
        def _():
            send[c, slot] = encode(term(block, c))

        z_copy(c, d, j, slot).start()

    def first(c):
        @pl.loop(0, nz - 1 - m)
        def _(j):
            move(c, way, j, j, m > 0)

    def second(c):
        @pl.loop(0, m)
        def _(j):
            move(c, 1 - way, j, nz - 1 - m + j, True)

    def finish(c):
        wg[c] = term(z, c)
        for d in range(2):
            j = nz - 1 - z if d == 0 else z

            @pl.when(z > 0 if d == 0 else z < nz - 1)
            def _():
                z_copy(c, d, j, 0).wait_recv()
                wg[c] = wg[c] + decode(recv[c, d, j])

        wg[c] = wg[c] * down

    step_f = 512 if feats % 512 == 0 else feats

    def partial(ka, kb, put):
        @pl.loop(0, feats // step_f)
        def _(i):
            cols = pl.ds(pl.multiple_of(i * step_f, step_f), step_f)
            acc = jnp.zeros((2 * rows, step_f), F32)
            for c in range(lc):
                lhs = jnp.concatenate([near_ref(c, ka)[...], near_ref(c, kb)[...]], axis=0)
                acc = acc + lax.dot_general(
                    lhs, wv[c, cols, :], (((1,), (1,)), ((), ())), preferred_element_type=F32
                )
            put(cols, acc)

    def ig_copy(i):
        return rcopy(igs.at[i], igr.at[i], ss_ig.at[i], rs_ig.at[i], dp_dev(1))

    x_copy = rcopy(xs.at[0], xr, ss_ig.at[2], rs_ig.at[2], dp_dev(2))

    def put_pair(cols, acc):
        igs[0, :, cols] = acc[:rows]
        igs[1, :, cols] = acc[rows:]

    def put_own(cols, acc):
        xs[0, :, cols] = acc[:rows] + igr[0, :, cols]
        xs[1, :, cols] = acc[rows:] + igr[1, :, cols]

    for c in range(lc):
        for k in range(4):
            y_copy(c, k).wait_recv()
        first(c)
        if c + 2 < lc:
            forward(c + 2)
        if c == lc - 2:
            wcopy.wait()
            partial(3, 1, put_pair)
            ig_copy(0).start()
            ig_copy(1).start()
        if c > 0:
            second(c - 1)
        if c > 1:
            finish(c - 2)
    ig_copy(0).wait_recv()
    ig_copy(1).wait_recv()
    partial(2, 0, put_own)
    x_copy.start()
    finish(lc - 2)
    second(lc - 1)
    x_copy.wait_recv()
    ig[...] = (xs[1] + xr[...]).astype(BF16)
    finish(lc - 1)

    for c in range(lc):
        for k in range(4):
            if k:
                dp_copy(c, k).wait_send()
            y_copy(c, k).wait_send()

        @pl.loop(0, nz - 1)
        def _(j):
            z_copy(c, 0, 0, j).wait_send()

    for e in (e_y, e_own1, e_own2, e_far1, e_far2, e_on1, e_on1f, ig_copy(0), ig_copy(1), x_copy):
        e.wait_send()
    for i in range(3):
        pk_copy(i, y_dev).wait_send()

    @pl.loop(1, nz)
    def _(d):
        pz_copy(d).wait_send()


def local(encoded, cotangents, weights):
    ndp, nseq = lax.axis_size("dp"), lax.axis_size("seq")
    nz = nseq // 2
    layers, _, rows, parts, units = cotangents.shape
    feats = encoded.shape[2]
    dl = feats // nseq
    el = units // ndp
    lc = layers * parts
    cot = cotangents[:, 0].reshape(layers, rows, parts, ndp, el)
    cot = cot.transpose(3, 0, 2, 1, 4).reshape(ndp, lc, rows, el)
    enc = encoded[0].reshape(rows, nz, 2, dl).transpose(2, 1, 3, 0)
    w = weights.reshape(lc, feats, el)
    dma = pltpu.SemaphoreType.DMA
    ig, wg = pl.pallas_call(
        lambda *refs: kernel(ndp, nseq, *refs),
        out_shape=(
            jax.ShapeDtypeStruct((rows, feats), BF16),
            jax.ShapeDtypeStruct((lc, dl, el), F32),
        ),
        in_specs=[
            pl.BlockSpec(memory_space=pltpu.VMEM),
            pl.BlockSpec(memory_space=pltpu.VMEM),
            pl.BlockSpec(memory_space=pl.ANY),
        ],
        out_specs=(pl.BlockSpec(memory_space=pltpu.VMEM), pl.BlockSpec(memory_space=pltpu.VMEM)),
        scratch_shapes=[
            pltpu.VMEM((lc, ndp - 1, rows, el), BF16),
            pltpu.VMEM((lc, ndp, rows, el), BF16),
            pltpu.VMEM((2 * ndp, nz, dl, rows), BF16),
            pltpu.VMEM((lc, 2, nz - 1, dl, el), BF16),
            pltpu.VMEM((lc, nz - 1, dl, el), BF16),
            pltpu.VMEM((lc, feats, el), BF16),
            pltpu.VMEM((2, rows, feats), F32),
            pltpu.VMEM((2, rows, feats), F32),
            pltpu.VMEM((2, rows, feats), F32),
            pltpu.VMEM((rows, feats), F32),
            pltpu.VMEM((4, 8, 128), F32),
            pltpu.VMEM((3, 8, 128), F32),
            pltpu.VMEM((nz, 8, 128), F32),
            dma,
            dma((lc, 8)),
            dma((lc, 8)),
            dma((8,)),
            dma((8,)),
            dma((lc, nz - 1)),
            dma((lc, 2, nz - 1)),
            dma((3,)),
            dma((3,)),
            dma((3,)),
            dma((3,)),
            dma((nz,)),
            dma((nz,)),
        ],
        compiler_params=pltpu.CompilerParams(
            collective_id=0, has_side_effects=True, vmem_limit_bytes=56 * 2**20
        ),
    )(cot, enc, w)
    weight_grad = wg.reshape(layers, parts, dl, el).transpose(2, 0, 1, 3)
    return (ig[None], weight_grad)


def solution(mesh):
    return jax.shard_map(
        local,
        mesh=mesh,
        in_specs=(
            P("dp", "seq", None),
            P(None, "dp", "seq", None, None),
            P(None, None, None, "dp"),
        ),
        out_specs=(P("dp", "seq", None), P("seq", None, None, "dp")),
        check_vma=False,
    )
```

time: 435 us -> 152 us (0.35)
  the two profiles are of different devices: /device:TPU:0 before, /device:TPU:12 now
where the time goes in v2:
time: 152 us
  Pallas kernels  139 us (91%)
  local copies, waits for them, and re-layouts  12.7 us (8%)
    pallas_call x1, Pallas kernels, local(): pl.pallas_call(lambda *refs: kernel(ndp, nseq, *refs), out_shape=(jax.Sha...  139 us
    another operation x2, local copies, waits for them, and re-layouts, local(): cot = cotangents[:, 0].reshape(layers, rows, parts, ndp, el)  5.15 us
    reshape x1, local copies, waits for them, and re-layouts, local(): weight_grad = wg.reshape(layers, parts, dl, el).transpose(2, 0, 1, 3)  4.59 us

profile of v2, /device:TPU:12, one launch (start us, length us, event | category | flops | bytes accessed | tf_op | source)
XLA Modules:
  0.0 152.1 jit_solution(12892076175265062221)
XLA Ops:
  0.6 1.3 copy.8
  1.9 0.8 copy.14
  2.8 3.2 %reshape_squeeze.6 = bf16[2,128,2,4,512]{4,3,2,1,0:T(4,128)(2,1)S(1)} reshape(bf16[2,1,128,2,2048]{4,3,2,1,0:T(2,128)(2,1)} %param.4) | data formatting | bytes 4194304 | tf_op jit(solution)/shard_map/reshape;squeeze | solution.py:303
  5.9 2.0 %copy.7 = bf16[2,128,2,4,512]{4,1,2,0,3:T(8,128)(2,1)} copy(bf16[2,128,2,4,512]{4,3,2,1,0:T(4,128)(2,1)S(1)} %reshape_squeeze.6) | data formatting | bytes 4194304 | tf_op jit(solution)/shard_map/reshape;squeeze | solution.py:303
  7.9 138.8 %shard_map.50 = (bf16[128,2048]{1,0:T(8,128)(2,1)}, f32[4,256,512]{2,1,0:T(8,128)}) custom-call(bf16[4,4,128,512]{3,2,1,0:T(8,128)(2,1)} %bitcast.14, bf16[2,4,256,128]{3,2,1,0:T(8,128)(2,1)} %bitcast.18, bf16[4,2048,512]{2,1,0:T(8,128)(2,1)} %bitcast.13), custom_call_target="tpu_custom_call" | custom-call | tf_op jit(solution)/shard_map/pallas_call | solution.py:308
  146.8 0.0 copy-start
  146.8 4.6 %copy.13 = f32[2,2,256,512]{3,1,0,2:T(2,128)} copy(f32[2,2,256,512]{3,2,1,0:T(8,128)} %bitcast.16) | data formatting | bytes 4194304 | tf_op jit(solution)/shard_map/reshape | solution.py:352
  151.3 0.0 copy-done
  151.4 0.8 copy.16
Async XLA Ops:
  146.8 4.6 %copy-start = (bf16[128,2048]{1,0:T(8,128)(2,1)S(1)}, bf16[128,2048]{1,0:T(8,128)(2,1)}, u32[]{:S(2)}) copy-start(bf16[128,2048]{1,0:T(8,128)(2,1)} %get-tuple-element.4) | copy-start | bytes 1572868

commit v3 on v2

--- a/solution.py
+++ b/solution.py
@@ -90,9 +90,11 @@
     dp_copy(0, 3).start()
     e_own1.start()
     wcopy.start()
-    for c in range(1, lc):
-        for k in (1, 2, 3):
-            dp_copy(c, k).start()
+
+    def dp_start(c):
+        if c < lc:
+            for k in (2, 3, 1):
+                dp_copy(c, k).start()
 
     def cot_peak(i, m):
         return jnp.maximum(m, jnp.max(jnp.abs(cot[i // lc, i % lc].astype(F32)), axis=0, keepdims=True))
@@ -115,6 +117,7 @@
     pks[0] = tile
     pk_copy(0, dp_dev(1)).start()
 
+    dp_start(1)
     dp_copy(0, 1).wait_recv()
     y_copy(0, 1).start()
     pk_stage(0)
@@ -127,6 +130,7 @@
     for k in (2, 3):
         dp_copy(0, k).wait_recv()
         y_copy(0, k).start()
+    dp_start(2)
     pk_stage(1)
     pk_copy(2, y_dev).start()
 
@@ -135,6 +139,7 @@
             if k:
                 dp_copy(c, k).wait_recv()
             y_copy(c, k).start()
+        dp_start(c + 2)
 
     def pz_copy(d):
         return rcopy(pks.at[3], pkz.at[d], ss_pz.at[d], rs_pz.at[d], z_dev((z + d) % nz))
@@ -195,6 +200,7 @@
         @pl.when(jnp.logical_not(has_prev))
         def _():
             send[c, slot] = encode(term(block, c))
+
 
         z_copy(c, d, j, slot).start()
 
@@ -253,19 +259,20 @@
         first(c)
         if c + 2 < lc:
             forward(c + 2)
-        if c == lc - 2:
+        if c == lc - 3:
             wcopy.wait()
             partial(3, 1, put_pair)
             ig_copy(0).start()
             ig_copy(1).start()
         if c > 0:
             second(c - 1)
+        if c == lc - 2:
+            ig_copy(0).wait_recv()
+            ig_copy(1).wait_recv()
+            partial(2, 0, put_own)
+            x_copy.start()
         if c > 1:
             finish(c - 2)
-    ig_copy(0).wait_recv()
-    ig_copy(1).wait_recv()
-    partial(2, 0, put_own)
-    x_copy.start()
     finish(lc - 2)
     second(lc - 1)
     x_copy.wait_recv()

time: 152 us -> 128 us (0.84)
  the two profiles are of different devices: /device:TPU:12 before, /device:TPU:0 now
where the time goes in v3:
time: 128 us; the launch traced here: 127 us
  Pallas kernels  114 us (89%)
  local copies, waits for them, and re-layouts  12.7 us (10%)
    pallas_call x1, Pallas kernels, local(): pl.pallas_call(lambda *refs: kernel(ndp, nseq, *refs), out_shape=(jax.Sha...  114 us
    another operation x2, local copies, waits for them, and re-layouts, local(): cot = cotangents[:, 0].reshape(layers, rows, parts, ndp, el)  5.15 us
    reshape x1, local copies, waits for them, and re-layouts, local(): weight_grad = wg.reshape(layers, parts, dl, el).transpose(2, 0, 1, 3)  4.59 us

profile of v3, /device:TPU:0, one launch (start us, length us, event | category | flops | bytes accessed | tf_op | source)
XLA Modules:
  0.0 127.5 jit_solution(9661798966548332779)
XLA Ops:
  0.6 1.3 %copy.8 = bf16[1,128,2048]{1,2,0:T(8,128)(2,1)S(1)} copy(bf16[1,128,2048]{2,1,0:T(8,128)(2,1)} %param.3) | data formatting | bytes 1048576 | tf_op args[0]
  1.9 0.8 copy.14
  2.8 3.2 %reshape_squeeze.6 = bf16[2,128,2,4,512]{4,3,2,1,0:T(4,128)(2,1)S(1)} reshape(bf16[2,1,128,2,2048]{4,3,2,1,0:T(2,128)(2,1)} %param.4) | data formatting | bytes 4194304 | tf_op jit(solution)/shard_map/reshape;squeeze | solution.py:310
  5.9 2.0 %copy.7 = bf16[2,128,2,4,512]{4,1,2,0,3:T(8,128)(2,1)} copy(bf16[2,128,2,4,512]{4,3,2,1,0:T(4,128)(2,1)S(1)} %reshape_squeeze.6) | data formatting | bytes 4194304 | tf_op jit(solution)/shard_map/reshape;squeeze | solution.py:310
  7.9 114.2 %shard_map.50 = (bf16[128,2048]{1,0:T(8,128)(2,1)}, f32[4,256,512]{2,1,0:T(8,128)}) custom-call(bf16[4,4,128,512]{3,2,1,0:T(8,128)(2,1)} %bitcast.14, bf16[2,4,256,128]{3,2,1,0:T(8,128)(2,1)} %bitcast.18, bf16[4,2048,512]{2,1,0:T(8,128)(2,1)} %bitcast.13), custom_call_target="tpu_custom_call" | custom-call | tf_op jit(solution)/shard_map/pallas_call | solution.py:315
  122.1 0.0 copy-start
  122.1 4.6 %copy.13 = f32[2,2,256,512]{3,1,0,2:T(2,128)} copy(f32[2,2,256,512]{3,2,1,0:T(8,128)} %bitcast.16) | data formatting | bytes 4194304 | tf_op jit(solution)/shard_map/reshape | solution.py:359
  126.7 0.0 copy-done
  126.7 0.8 copy.16
Async XLA Ops:
  122.1 4.6 %copy-start = (bf16[128,2048]{1,0:T(8,128)(2,1)S(1)}, bf16[128,2048]{1,0:T(8,128)(2,1)}, u32[]{:S(2)}) copy-start(bf16[128,2048]{1,0:T(8,128)(2,1)} %get-tuple-element.4) | copy-start | bytes 1572868

commit v4 on v3

--- a/solution.py
+++ b/solution.py
@@ -25,7 +25,8 @@
 def kernel(ndp, nseq, cot, enc, w, ig, wg, near, far, encs, recv, send, wv, igs, igr, xs, xr, pks, pkr, pkz,
            wsem, ss_cot, rs_cot, ss_enc, rs_enc, ss_z, rs_z, ss_ig, rs_ig, ss_pk, rs_pk, ss_pz, rs_pz):
     nz = nseq // 2
-    _, lc, rows, el = cot.shape
+    lc, rows, units = cot.shape
+    el = units // ndp
     dl = enc.shape[2]
     feats = w.shape[1]
     tokens = rows * nseq * ndp
@@ -73,11 +74,14 @@
     e_on1 = enc_copy(6, encs.at[4], dp_dev(1))
     e_on1f = enc_copy(7, encs.at[5], dp_dev(1))
 
+    def head(i):
+        return pl.ds(pl.multiple_of(i * el, el), el)
+
     def near_ref(c, k):
-        return cot.at[me, c] if k == 0 else near.at[c, k - 1]
+        return cot.at[c, :, head(me)] if k == 0 else near.at[c, k - 1]
 
     def dp_copy(c, k):
-        return rcopy(cot.at[dps[k], c], near.at[c, k - 1], ss_cot.at[c, k], rs_cot.at[c, k], dp_dev(k))
+        return rcopy(cot.at[c, :, head(dps[k])], near.at[c, k - 1], ss_cot.at[c, k], rs_cot.at[c, k], dp_dev(k))
 
     def y_copy(c, k):
         return rcopy(near_ref(c, k), far.at[c, k], ss_cot.at[c, 4 + k], rs_cot.at[c, 4 + k], y_dev)
@@ -97,7 +101,7 @@
                 dp_copy(c, k).start()
 
     def cot_peak(i, m):
-        return jnp.maximum(m, jnp.max(jnp.abs(cot[i // lc, i % lc].astype(F32)), axis=0, keepdims=True))
+        return jnp.maximum(m, jnp.max(jnp.abs(cot[i // ndp, :, head(i % ndp)].astype(F32)), axis=0, keepdims=True))
 
     def enc_peak(i, m):
         return jnp.maximum(m, jnp.max(jnp.abs(enc[i // nz, i % nz].astype(F32)), axis=0, keepdims=True))
@@ -177,7 +181,7 @@
         lhs = jnp.concatenate([enc[y, b]] + [encs[s, b] for s in range(1, 2 * ndp)], axis=1)
         pieces = []
         for k in range(ndp):
-            pieces += [cot[me, c] if k == 0 else near[c, k - 1], far[c, k]]
+            pieces += [cot[c, :, head(me)] if k == 0 else near[c, k - 1], far[c, k]]
         rhs = jnp.concatenate(pieces, axis=0)
         t = jnp.dot(lhs, rhs, preferred_element_type=F32)
         return t * up_e * up_c
@@ -273,8 +277,8 @@
             x_copy.start()
         if c > 1:
             finish(c - 2)
+    second(lc - 1)
     finish(lc - 2)
-    second(lc - 1)
     x_copy.wait_recv()
     ig[...] = (xs[1] + xr[...]).astype(BF16)
     finish(lc - 1)
@@ -307,8 +311,7 @@
     dl = feats // nseq
     el = units // ndp
     lc = layers * parts
-    cot = cotangents[:, 0].reshape(layers, rows, parts, ndp, el)
-    cot = cot.transpose(3, 0, 2, 1, 4).reshape(ndp, lc, rows, el)
+    cot = cotangents[:, 0].transpose(0, 2, 1, 3).reshape(lc, rows, units)
     enc = encoded[0].reshape(rows, nz, 2, dl).transpose(2, 1, 3, 0)
     w = weights.reshape(lc, feats, el)
     dma = pltpu.SemaphoreType.DMA

time: 128 us -> 124 us (0.969)
  local copies, waits for them, and re-layouts: 12.7 us -> 9.88 us
    another operation x2 -> x0, local copies, waits for them, and re-layouts: 5.15 us -> none  [local(): cot = cotangents[:, 0].reshape(layers, rows, parts, ndp, el)]
    transpose x0 -> x1, local copies, waits for them, and re-layouts: none -> 2.2 us  [local(): cot = cotangents[:, 0].transpose(0, 2, 1, 3).reshape(lc, rows, units)]
where the time goes in v4:
time: 124 us
  Pallas kernels  114 us (92%)
  local copies, waits for them, and re-layouts  9.88 us (8%)
    pallas_call x1, Pallas kernels, local(): pl.pallas_call(lambda *refs: kernel(ndp, nseq, *refs), out_shape=(jax.Sha...  114 us
    reshape x1, local copies, waits for them, and re-layouts, local(): weight_grad = wg.reshape(layers, parts, dl, el).transpose(2, 0, 1, 3)  4.59 us

profile of v4, /device:TPU:0, one launch (start us, length us, event | category | flops | bytes accessed | tf_op | source)
XLA Modules:
  0.0 124.2 jit_solution(14355551282705796751)
XLA Ops:
  0.6 0.0 copy-start
  0.6 1.5 %copy.8 = bf16[1,128,2048]{1,2,0:T(8,128)(2,1)S(1)} copy(bf16[1,128,2048]{2,1,0:T(8,128)(2,1)} %param.3) | data formatting | bytes 1048576 | tf_op args[0]
  2.1 0.8 copy.14
  2.9 0.0 copy-done
  2.9 2.2 %copy.7 = bf16[2,2,128,2048]{3,2,1,0:T(8,128)(2,1)} copy(bf16[2,2,128,2048]{3,1,2,0:T(2,128)(2,1)S(1)} %bitcast.16) | data formatting | bytes 4194304 | tf_op jit(solution)/shard_map/transpose | solution.py:314
  5.1 113.7 %shard_map.50 = (bf16[128,2048]{1,0:T(8,128)(2,1)}, f32[4,256,512]{2,1,0:T(8,128)}) custom-call(bf16[4,128,2048]{2,1,0:T(8,128)(2,1)} %bitcast.15, bf16[2,4,256,128]{3,2,1,0:T(8,128)(2,1)} %bitcast.20, bf16[4,2048,512]{2,1,0:T(8,128)(2,1)} %bitcast.14), custom_call_target="tpu_custom_call" | custom-call | tf_op jit(solution)/shard_map/pallas_call | solution.py:318
  118.8 0.0 copy-start.1
  118.8 4.6 %copy.13 = f32[2,2,256,512]{3,1,0,2:T(2,128)} copy(f32[2,2,256,512]{3,2,1,0:T(8,128)} %bitcast.18) | data formatting | bytes 4194304 | tf_op jit(solution)/shard_map/reshape | solution.py:362
  123.4 0.0 copy-done.1
  123.4 0.8 copy.16
Async XLA Ops:
  0.6 2.3 %copy-start = (bf16[2,1,128,2,2048]{4,3,2,1,0:T(2,128)(2,1)S(1)}, bf16[2,1,128,2,2048]{4,3,2,1,0:T(2,128)(2,1)}, u32[]{:S(2)}) copy-start(bf16[2,1,128,2,2048]{4,3,2,1,0:T(2,128)(2,1)} %param.4) | copy-start | bytes 6291460
  118.8 4.6 %copy-start.1 = (bf16[128,2048]{1,0:T(8,128)(2,1)S(1)}, bf16[128,2048]{1,0:T(8,128)(2,1)}, u32[]{:S(2)}) copy-start(bf16[128,2048]{1,0:T(8,128)(2,1)} %get-tuple-element.4) | copy-start | bytes 1572868
